TPU v7x, 256 devices: a whole 4x4x8 slice. The times are simulated.
256 devices in a mesh: dp: 32 (over y, z_hi, core), tensor: 8 (over z_lo, x).
Axes of the slice: x: 4, y: 4, z: 8 (z_hi: 4, z_lo: 2; z = z_hi * 2 + z_lo), core: 2. Of those that a mesh axis runs over, the one named last changes fastest.
Arguments:
- cotangent: bfloat16 [32768, 4096], P(('dp', 'tensor')), may hold values from -24 to 24
- features: bfloat16 [32768, 1024], P(('dp', 'tensor')), may hold values from -24 to 24
- normed: bfloat16 [32768, 1024], P(('dp', 'tensor')), may hold values from -24 to 24
- pre_hidden: bfloat16 [32768, 4096], P('dp', 'tensor'), may hold values from -6 to 6
- pre_inner: bfloat16 [32768, 4096], P('dp', 'tensor'), may hold values from -8 to 8
- w_first: bfloat16 [1024, 4096], P(None, 'tensor'), may hold values from -0.1875 to 0.1875
- w_second: bfloat16 [4096, 4096], P('tensor'), may hold values from -0.09375 to 0.09375
- w_down: bfloat16 [4096, 1024], P('tensor'), may hold values from -0.09375 to 0.09375
Outputs:
- grad_second: float32 [4096, 4096], P('tensor', 'dp')
- grad_first: float32 [1024, 4096], P('dp', 'tensor')
- grad_down: float32 [4096, 1024], P('tensor', 'dp')
- grad_up: float32 [1024, 4096], P('dp', 'tensor')
- encoder_cotangent: bfloat16 [32768, 1024], P(('dp', 'tensor'))
All inputs are finite; a program needn't handle non-finite values.
Results may differ from a plain program's by a relative error of at most 0.02.
Values may be sent and summed in bfloat16 or wider, within the bound.
A program may use at most 128 MiB of HBM per device.

v0:
```python
import math
import jax
import jax.numpy as jnp
from jax import lax
from jax.sharding import PartitionSpec as P


def normal_cdf(value):
    return 0.5 * (1.0 + jax.scipy.special.erf(value * (1.0 / math.sqrt(2.0))))


def normal_pdf(value):
    return jnp.exp(-0.5 * value * value) * (1.0 / math.sqrt(2.0 * math.pi))


def over_rows(left, right):
    return lax.dot_general(
        left, right, (((0,), (0,)), ((), ())), preferred_element_type=jnp.float32
    )


def over_cols(left, right):
    return lax.dot_general(
        left, right, (((1,), (1,)), ((), ())), preferred_element_type=jnp.float32
    )


def on_device(cotangent, features, normed, pre_hidden, pre_inner, w_first, w_second, w_down):
    tok_rows = cotangent.shape[0]
    tensor_count = lax.axis_size("tensor")
    replica_count = lax.axis_size("dp")
    factor = 1.0 / math.sqrt(tok_rows * tensor_count * replica_count)
    pre_value = pre_hidden.astype(jnp.float32)
    hidden_act = (pre_value * normal_cdf(pre_value)).astype(jnp.bfloat16)
    slope = normal_cdf(pre_value) + pre_value * normal_pdf(pre_value)
    piece = lax.all_gather(cotangent, "tensor", axis=0, tiled=True)
    accum = over_rows(hidden_act, piece)
    d_hidden = over_cols(piece, w_second)
    accum, d_hidden = (accum, d_hidden)
    grad_second = lax.psum_scatter(accum * factor, "dp", scatter_dimension=1, tiled=True)
    d_pre = (d_hidden * slope).astype(jnp.bfloat16)
    feat_all, norm_all = (
        lax.all_gather(features, "tensor", axis=0, tiled=True),
        lax.all_gather(normed, "tensor", axis=0, tiled=True),
    )
    first_term = over_rows(feat_all, d_pre) * factor
    own_rows = lax.psum_scatter(
        over_cols(d_pre, w_first).astype(jnp.bfloat16), "tensor", scatter_dimension=0, tiled=True
    )
    cot_all = lax.all_gather(own_rows, "tensor", axis=0, tiled=True)
    inner_value = pre_inner.astype(jnp.float32)
    sig = jax.nn.sigmoid(1.702 * inner_value)
    inner_act = (inner_value * sig).astype(jnp.bfloat16)
    down_term = over_rows(cot_all, inner_act) * factor
    d_act = over_cols(cot_all, w_down)
    d_inner = (d_act * (sig + 1.702 * inner_value * sig * (1.0 - sig))).astype(jnp.bfloat16)
    up_term = over_rows(norm_all, d_inner) * factor
    grad_first, grad_up, down_rows = (
        lax.psum_scatter(first_term, "dp", scatter_dimension=0, tiled=True),
        lax.psum_scatter(up_term, "dp", scatter_dimension=0, tiled=True),
        lax.psum_scatter(down_term, "dp", scatter_dimension=0, tiled=True),
    )
    return (grad_second, grad_first, down_rows.T, grad_up, own_rows)


def solution(mesh):
    return jax.shard_map(
        on_device,
        mesh=mesh,
        in_specs=(
            P(("dp", "tensor"), None),
            P(("dp", "tensor"), None),
            P(("dp", "tensor"), None),
            P("dp", "tensor"),
            P("dp", "tensor"),
            P(None, "tensor"),
            P("tensor", None),
            P("tensor", None),
        ),
        out_specs=(
            P("tensor", "dp"),
            P("dp", "tensor"),
            P("tensor", "dp"),
            P("dp", "tensor"),
            P(("dp", "tensor"), None),
        ),
        check_vma=False,
    )
```

profile of v0, /device:TPU:2, one launch (start us, length us, event | category | flops | bytes accessed | tf_op | source)
XLA Modules:
  0.0 712.9 jit_solution(7468318923826055815)
XLA Ops:
  7.2 0.0 copy-start
  7.2 0.0 all-gather.5.cloned.1.call-start
  7.2 0.7 all-gather.5.cloned.1.call-update
  7.9 0.0 reduce-scatter.12.cloned.1.call-start
  8.0 97.1 %all-gather.5.cloned.1.call-done = bf16[1024,4096]{1,0:T(8,128)(2,1)} async-done(((bf16[128,4096]{1,0:T(8,128)(2,1)}), bf16[1024,4096]{1,0:T(8,128)(2,1)}) %all-gather.5.cloned.1.call-update) | async-done | bytes 8388624 | tf_op jit(solution)/shard_map/all_gather | solution.py:36
  105.0 10.0 %fusion.18 = bf16[1024,512]{1,0:T(8,128)(2,1)S(1)} fusion(bf16[1024,512]{1,0:T(8,128)(2,1)} %param.11, bf16[1024,4096]{1,0:T(8,128)(2,1)} %all-gather.5.cloned.1.call-done, bf16[512,4096]{1,0:T(8,128)(2,1)} %param.14), kind=kOutput, calls=%fused_computation.26 | convolution fusion | flops 4300734464 | bytes 14680064 | tf_op jit(solution)/shard_map/dot_general | solution.py:23
  115.0 0.0 copy-start.2
  115.0 1.0 copy-done.2
  116.0 0.0 copy-done
  116.0 2.7 convolution_convert_fusion
  118.7 0.0 reduce-scatter.12.cloned.1.call-update
  118.7 0.0 all-gather.7.cloned.1.call-start
  118.7 0.7 all-gather.7.cloned.1.call-update
  119.4 0.0 all-gather.9.cloned.1.call-start
  119.5 42.7 %reduce-scatter.12.cloned.1.call-done = bf16[128,1024]{1,0:T(8,128)(2,1)} async-done(((bf16[1024,1024]{1,0:T(8,128)(2,1)}), bf16[128,1024]{1,0:T(8,128)(2,1)}) %reduce-scatter.12.cloned.1.call-update) | async-done | bytes 262160 | tf_op jit(solution)/shard_map/reduce_scatter | solution.py:47
  162.2 0.0 all-gather.9.cloned.1.call-update
  162.2 0.0 all-gather.11.cloned.1.call-start
  162.3 0.5 all-gather.11.cloned.1.call-update
  162.8 0.0 reduce-scatter.16.cloned.1.call-start
  162.8 44.7 %all-gather.7.cloned.1.call-done = bf16[1024,1024]{1,0:T(8,128)(2,1)} async-done(((bf16[128,1024]{1,0:T(8,128)(2,1)}), bf16[1024,1024]{1,0:T(8,128)(2,1)}) %all-gather.7.cloned.1.call-update) | async-done | bytes 2097168 | tf_op jit(solution)/shard_map/all_gather | solution.py:43
  207.5 3.2 multiply_bitcast_fusion.1
  210.7 1.8 copy.17
  212.6 0.0 copy-start.3
  212.6 0.0 reduce-scatter.16.cloned.1.call-update
  212.6 0.0 reduce-scatter.14.cloned.1.call-start
  212.7 40.5 %all-gather.9.cloned.1.call-done = bf16[1024,1024]{1,0:T(8,128)(2,1)} async-done(((bf16[128,1024]{1,0:T(8,128)(2,1)}), bf16[1024,1024]{1,0:T(8,128)(2,1)}) %all-gather.9.cloned.1.call-update) | async-done | bytes 2097168 | tf_op jit(solution)/shard_map/all_gather | solution.py:50
  253.1 0.0 copy-done.3
  253.1 4.3 convolution_multiply_fusion.1
  257.5 0.0 reduce-scatter.14.cloned.1.call-update
  257.5 0.0 reduce-scatter.18.cloned.1.call-start
  257.5 40.6 %all-gather.11.cloned.1.call-done = bf16[1024,1024]{1,0:T(8,128)(2,1)} async-done(((bf16[128,1024]{1,0:T(8,128)(2,1)}), bf16[1024,1024]{1,0:T(8,128)(2,1)}) %all-gather.11.cloned.1.call-update) | async-done | bytes 2097168 | tf_op jit(solution)/shard_map/all_gather | solution.py:44
  298.2 5.7 multiply_bitcast_fusion
  303.9 1.9 copy.19
  305.7 0.0 copy-start.1
  305.7 0.0 reduce-scatter.18.cloned.1.call-update
  305.8 0.2 reduce-scatter.10.cloned.1.call-start
  306.0 1.0 copy-done.1
  307.0 10.4 %convolution_multiply_fusion = f32[512,4096]{1,0:T(8,128)} fusion(bf16[1024,4096]{1,0:T(8,128)(2,1)} %all-gather.5.cloned.1.call-done, bf16[1024,512]{1,0:T(8,128)(2,1)S(1)} %copy-done.1), kind=kOutput, calls=%fused_computation | convolution fusion | flops 4300210176 | bytes 17825792 | tf_op jit(solution)/shard_map/dot_general | solution.py:17
  317.3 0.0 reduce-scatter.10.cloned.1.call-update
  317.4 78.2 %reduce-scatter.16.cloned.1.call-done = f32[32,512]{1,0:T(8,128)} async-done(((f32[1024,512]{1,0:T(8,128)}), f32[32,512]{1,0:T(8,128)}) %reduce-scatter.16.cloned.1.call-update) | async-done | bytes 65552
  395.5 93.5 %reduce-scatter.14.cloned.1.call-done = f32[32,512]{1,0:T(8,128)} async-done(((f32[1024,512]{1,0:T(8,128)}), f32[32,512]{1,0:T(8,128)}) %reduce-scatter.14.cloned.1.call-update) | async-done | bytes 65552 | tf_op jit(solution)/shard_map/reduce_scatter | solution.py:61
  489.0 93.5 %reduce-scatter.18.cloned.1.call-done = f32[32,512]{1,0:T(8,128)} async-done(((f32[1024,512]{1,0:T(8,128)}), f32[32,512]{1,0:T(8,128)}) %reduce-scatter.18.cloned.1.call-update) | async-done | bytes 65552
  582.6 123.8 %reduce-scatter.10.cloned.1.call-done = f32[512,128]{1,0:T(8,128)} async-done(((f32[512,4096]{1,0:T(8,128)}), f32[512,128]{1,0:T(8,128)}) %reduce-scatter.10.cloned.1.call-update) | async-done | bytes 262160 | tf_op jit(solution)/shard_map/reduce_scatter | solution.py:40
Async XLA Ops:
  7.2 108.8 %copy-start = (bf16[1024,512]{1,0:T(8,128)(2,1)S(1)}, bf16[1024,512]{1,0:T(8,128)(2,1)}, u32[]{:S(2)}) copy-start(bf16[1024,512]{1,0:T(8,128)(2,1)} %param.13) | copy-start | bytes 3145732
  7.2 97.9 %all-gather.5.cloned.1.call-start = ((), (), s32[]{:S(2)}) async-start(), calls=%async_computation.5 | async-start | bytes 9437184 | tf_op jit(solution)/shard_map/all_gather | solution.py:36
  7.9 154.3 %reduce-scatter.12.cloned.1.call-start = ((), (), s32[]{:S(2)}) async-start(), calls=%async_computation.8 | async-start | bytes 2359296 | tf_op jit(solution)/shard_map/reduce_scatter | solution.py:47
  115.0 1.0 copy-start.2
  118.7 88.9 %all-gather.7.cloned.1.call-start = ((), (), s32[]{:S(2)}) async-start(), calls=%async_computation.7 | async-start | bytes 2359296 | tf_op jit(solution)/shard_map/all_gather | solution.py:43
  119.4 133.7 %all-gather.9.cloned.1.call-start = ((), (), s32[]{:S(2)}) async-start(), calls=%async_computation.9 | async-start | bytes 2359296 | tf_op jit(solution)/shard_map/all_gather | solution.py:50
  162.2 135.9 %all-gather.11.cloned.1.call-start = ((), (), s32[]{:S(2)}) async-start(), calls=%async_computation.11 | async-start | bytes 2359296 | tf_op jit(solution)/shard_map/all_gather | solution.py:44
  162.8 232.7 %reduce-scatter.16.cloned.1.call-start = ((), (), s32[]{:S(2)}) async-start(), calls=%async_computation.12 | async-start | bytes 2162688
  212.6 40.6 %copy-start.3 = (bf16[1024,512]{1,0:T(8,128)(2,1)S(1)}, bf16[1024,512]{1,0:T(8,128)(2,1)}, u32[]{:S(2)}) copy-start(bf16[1024,512]{1,0:T(8,128)(2,1)} %param.12) | copy-start | bytes 3145732
  212.6 276.4 %reduce-scatter.14.cloned.1.call-start = ((), (), s32[]{:S(2)}) async-start(), calls=%async_computation.10 | async-start | bytes 2162688 | tf_op jit(solution)/shard_map/reduce_scatter | solution.py:61
  257.5 325.1 %reduce-scatter.18.cloned.1.call-start = ((), (), s32[]{:S(2)}) async-start(), calls=%async_computation.13 | async-start | bytes 2162688
  305.7 1.2 copy-start.1
  305.8 400.6 %reduce-scatter.10.cloned.1.call-start = ((), (), s32[]{:S(2)}) async-start(), calls=%async_computation.6 | async-start | bytes 8650752 | tf_op jit(solution)/shard_map/reduce_scatter | solution.py:40
Sparse Core Ops, SparseCore 0:
  9.8 95.2 all-gather.4
  118.8 43.3 reduce-scatter.11
  164.0 43.5 all-gather.6
  209.8 43.3 all-gather.8
  254.8 43.3 all-gather.10
  302.4 93.0 reduce-scatter.15
  399.9 89.0 reduce-scatter.13
  493.5 89.0 reduce-scatter.17
  587.2 119.1 reduce-scatter.9
where the time goes:
time: 713 us
  waiting for transfers between devices  657 us (92%)
  matrix products  36.2 us (5%)
  between operations  13.9 us (2%)
    unnamed x11, waiting for transfers between devices  174 us
    reduce_scatter x1, waiting for transfers between devices, on_device(): lax.psum_scatter(accum * factor, 'dp', scatter_dimension=1, tiled=True)  124 us
    all_gather x1, waiting for transfers between devices, on_device(): piece = lax.all_gather(cotangent, 'tensor', axis=0, tiled=True)  97.1 us
    reduce_scatter x1, waiting for transfers between devices, on_device(): lax.psum_scatter(down_term, 'dp', scatter_dimension=0, tiled=True)  93.5 us
    all_gather x1, waiting for transfers between devices, on_device(): lax.all_gather(features, 'tensor', axis=0, tiled=True)  44.7 us
    reduce_scatter x1, waiting for transfers between devices, on_device(): lax.psum_scatter(over_cols(d_pre, w_first).astype(jnp.bfloat16), 'tensor'...  42.7 us
    all_gather x1, waiting for transfers between devices, on_device(): lax.all_gather(normed, 'tensor', axis=0, tiled=True)  40.6 us
    all_gather x1, waiting for transfers between devices, on_device(): cot_all = lax.all_gather(own_rows, 'tensor', axis=0, tiled=True)  40.5 us
  transfers between devices with their start and end apart: 9, of which 9 were waited for; matrix products, arithmetic and copies ran while one was open for 4% of the time, Pallas kernels for 0%

commit v1 on v0

--- a/solution.py
+++ b/solution.py
@@ -47,7 +47,9 @@
     own_rows = lax.psum_scatter(
         over_cols(d_pre, w_first).astype(jnp.bfloat16), "tensor", scatter_dimension=0, tiled=True
     )
-    cot_all = lax.all_gather(own_rows, "tensor", axis=0, tiled=True)
+    cot_all = jnp.concatenate(
+        lax.all_to_all(jnp.stack([own_rows] * lax.axis_size("tensor")), "tensor", 0, 0), axis=0
+    )
     inner_value = pre_inner.astype(jnp.float32)
     sig = jax.nn.sigmoid(1.702 * inner_value)
     inner_act = (inner_value * sig).astype(jnp.bfloat16)

time: 713 us -> 678 us (0.951)
  waiting for transfers between devices: 657 us -> 610 us
  starting transfers between devices: 0.54 us -> 8.26 us
    all_gather x1 -> x0, waiting for transfers between devices: 40.5 us -> none  [on_device(): cot_all = lax.all_gather(own_rows, 'tensor', axis=0, tiled=True)]
    all_to_all x0 -> x1, starting transfers between devices: none -> 7.79 us  [on_device(): lax.all_to_all(jnp.stack([own_rows] * lax.axis_size('tensor')), 'tensor',...]
    unnamed x11 -> x10, waiting for transfers between devices: 174 us -> 174 us
  transfers between devices with their start and end apart: 9 -> 9, of which waited for: 9 -> 8; matrix products, arithmetic and copies ran while one was open for 4% -> 4% of each run, Pallas kernels for 0% -> 0%
where the time goes in v1:
time: 678 us; the launch traced here: 677 us
  waiting for transfers between devices  610 us (90%)
  matrix products  36.2 us (5%)
  between operations  14.2 us (2%)
  local copies, waits for them, and re-layouts  9.29 us (1%)
  starting transfers between devices  8.26 us (1%)
    unnamed x10, waiting for transfers between devices  174 us
    reduce_scatter x1, waiting for transfers between devices, on_device(): lax.psum_scatter(accum * factor, 'dp', scatter_dimension=1, tiled=True)  124 us
    all_gather x1, waiting for transfers between devices, on_device(): piece = lax.all_gather(cotangent, 'tensor', axis=0, tiled=True)  97.1 us
    reduce_scatter x1, waiting for transfers between devices, on_device(): lax.psum_scatter(down_term, 'dp', scatter_dimension=0, tiled=True)  93.4 us
    all_gather x1, waiting for transfers between devices, on_device(): lax.all_gather(features, 'tensor', axis=0, tiled=True)  45.9 us
    reduce_scatter x1, waiting for transfers between devices, on_device(): lax.psum_scatter(over_cols(d_pre, w_first).astype(jnp.bfloat16), 'tensor'...  42.1 us
    all_gather x1, waiting for transfers between devices, on_device(): lax.all_gather(normed, 'tensor', axis=0, tiled=True)  33.7 us
    dot_general x4, matrix products, over_rows(): lax.dot_general(left, right, (((0,), (0,)), ((), ())), preferred_element_...  23.6 us
  transfers between devices with their start and end apart: 9, of which 8 were waited for; matrix products, arithmetic and copies ran while one was open for 4% of the time, Pallas kernels for 0%

profile of v1, /device:TPU:2, one launch (start us, length us, event | category | flops | bytes accessed | tf_op | source)
XLA Modules:
  0.0 677.5 jit_solution(6549187328880868910)
XLA Ops:
  7.2 0.0 copy-start
  7.2 0.0 all-gather.4.cloned.1.call-start
  7.2 0.7 all-gather.4.cloned.1.call-update
  7.9 0.0 reduce-scatter.12.cloned.1.call-start
  8.0 97.1 %all-gather.4.cloned.1.call-done = bf16[1024,4096]{1,0:T(8,128)(2,1)} async-done(((bf16[128,4096]{1,0:T(8,128)(2,1)}), bf16[1024,4096]{1,0:T(8,128)(2,1)}) %all-gather.4.cloned.1.call-update) | async-done | bytes 8388624 | tf_op jit(solution)/shard_map/all_gather | solution.py:36
  105.0 10.0 %fusion.18 = bf16[1024,512]{1,0:T(8,128)(2,1)S(1)} fusion(bf16[1024,512]{1,0:T(8,128)(2,1)} %param.11, bf16[1024,4096]{1,0:T(8,128)(2,1)} %all-gather.4.cloned.1.call-done, bf16[512,4096]{1,0:T(8,128)(2,1)} %param.14), kind=kOutput, calls=%fused_computation.26 | convolution fusion | flops 4300734464 | bytes 14680064 | tf_op jit(solution)/shard_map/dot_general | solution.py:23
  115.0 0.0 copy-start.2
  115.0 1.0 copy-done.2
  116.0 0.0 copy-done
  116.0 2.6 convolution_convert_fusion
  118.6 0.0 reduce-scatter.12.cloned.1.call-update
  118.7 0.0 all-gather.6.cloned.1.call-start
  118.7 0.7 all-gather.6.cloned.1.call-update
  119.4 0.0 all-gather.8.cloned.1.call-start
  119.4 0.5 all-gather.8.cloned.1.call-update
  120.0 42.1 %reduce-scatter.12.cloned.1.call-done = bf16[128,1024]{1,0:T(8,128)(2,1)} async-done(((bf16[1024,1024]{1,0:T(8,128)(2,1)}), bf16[128,1024]{1,0:T(8,128)(2,1)}) %reduce-scatter.12.cloned.1.call-update) | async-done | bytes 262160 | tf_op jit(solution)/shard_map/reduce_scatter | solution.py:47
  162.1 2.5 stack.2
  164.6 7.8 %all-to-all-start = ((bf16[8,128,1024]{2,1,0:T(8,128)(2,1)}), bf16[8,128,1024]{2,1,0:T(8,128)(2,1)}, u32[]{:S(2)}, u32[]{:S(2)}) async-start(bf16[8,128,1024]{2,1,0:T(8,128)(2,1)} %stack.2), calls=%async_computation.2 | async-start | bytes 4194304 | tf_op jit(solution)/shard_map/all_to_all | solution.py:51
  172.4 0.0 reduce-scatter.16.cloned.1.call-start
  172.4 45.9 %all-gather.6.cloned.1.call-done = bf16[1024,1024]{1,0:T(8,128)(2,1)} async-done(((bf16[128,1024]{1,0:T(8,128)(2,1)}), bf16[1024,1024]{1,0:T(8,128)(2,1)}) %all-gather.6.cloned.1.call-update) | async-done | bytes 2097168 | tf_op jit(solution)/shard_map/all_gather | solution.py:43
  218.2 3.2 multiply_bitcast_fusion.1
  221.4 1.8 copy.17
  223.3 0.0 copy-start.3
  223.3 0.0 reduce-scatter.16.cloned.1.call-update
  223.3 0.0 reduce-scatter.14.cloned.1.call-start
  223.4 0.0 all-to-all-done
  223.4 1.1 copy-done.3
  224.5 4.3 convolution_multiply_fusion.1
  228.8 0.0 reduce-scatter.14.cloned.1.call-update
  228.8 0.0 reduce-scatter.18.cloned.1.call-start
  228.9 33.7 %all-gather.8.cloned.1.call-done = bf16[1024,1024]{1,0:T(8,128)(2,1)} async-done(((bf16[128,1024]{1,0:T(8,128)(2,1)}), bf16[1024,1024]{1,0:T(8,128)(2,1)}) %all-gather.8.cloned.1.call-update) | async-done | bytes 2097168 | tf_op jit(solution)/shard_map/all_gather | solution.py:44
  262.6 5.7 multiply_bitcast_fusion
  268.3 1.9 copy.19
  270.2 0.0 copy-start.1
  270.2 0.0 reduce-scatter.18.cloned.1.call-update
  270.2 0.2 reduce-scatter.10.cloned.1.call-start
  270.4 1.0 copy-done.1
  271.4 10.4 %convolution_multiply_fusion = f32[512,4096]{1,0:T(8,128)} fusion(bf16[1024,4096]{1,0:T(8,128)(2,1)} %all-gather.4.cloned.1.call-done, bf16[1024,512]{1,0:T(8,128)(2,1)S(1)} %copy-done.1), kind=kOutput, calls=%fused_computation | convolution fusion | flops 4300210176 | bytes 17825792 | tf_op jit(solution)/shard_map/dot_general | solution.py:17
  281.7 0.0 reduce-scatter.10.cloned.1.call-update
  281.8 78.2 %reduce-scatter.16.cloned.1.call-done = f32[32,512]{1,0:T(8,128)} async-done(((f32[1024,512]{1,0:T(8,128)}), f32[32,512]{1,0:T(8,128)}) %reduce-scatter.16.cloned.1.call-update) | async-done | bytes 65552
  359.9 93.4 %reduce-scatter.14.cloned.1.call-done = f32[32,512]{1,0:T(8,128)} async-done(((f32[1024,512]{1,0:T(8,128)}), f32[32,512]{1,0:T(8,128)}) %reduce-scatter.14.cloned.1.call-update) | async-done | bytes 65552 | tf_op jit(solution)/shard_map/reduce_scatter | solution.py:63
  453.3 93.6 %reduce-scatter.18.cloned.1.call-done = f32[32,512]{1,0:T(8,128)} async-done(((f32[1024,512]{1,0:T(8,128)}), f32[32,512]{1,0:T(8,128)}) %reduce-scatter.18.cloned.1.call-update) | async-done | bytes 65552
  546.8 123.8 %reduce-scatter.10.cloned.1.call-done = f32[512,128]{1,0:T(8,128)} async-done(((f32[512,4096]{1,0:T(8,128)}), f32[512,128]{1,0:T(8,128)}) %reduce-scatter.10.cloned.1.call-update) | async-done | bytes 262160 | tf_op jit(solution)/shard_map/reduce_scatter | solution.py:40
Async XLA Ops:
  7.2 108.8 %copy-start = (bf16[1024,512]{1,0:T(8,128)(2,1)S(1)}, bf16[1024,512]{1,0:T(8,128)(2,1)}, u32[]{:S(2)}) copy-start(bf16[1024,512]{1,0:T(8,128)(2,1)} %param.13) | copy-start | bytes 3145732
  7.2 97.9 %all-gather.4.cloned.1.call-start = ((), (), s32[]{:S(2)}) async-start(), calls=%async_computation.6 | async-start | bytes 9437184 | tf_op jit(solution)/shard_map/all_gather | solution.py:36
  7.9 154.1 %reduce-scatter.12.cloned.1.call-start = ((), (), s32[]{:S(2)}) async-start(), calls=%async_computation.9 | async-start | bytes 2359296 | tf_op jit(solution)/shard_map/reduce_scatter | solution.py:47
  115.0 1.0 copy-start.2
  118.7 99.6 %all-gather.6.cloned.1.call-start = ((), (), s32[]{:S(2)}) async-start(), calls=%async_computation.8 | async-start | bytes 2359296 | tf_op jit(solution)/shard_map/all_gather | solution.py:43
  119.4 143.2 %all-gather.8.cloned.1.call-start = ((), (), s32[]{:S(2)}) async-start(), calls=%async_computation.11 | async-start | bytes 2359296 | tf_op jit(solution)/shard_map/all_gather | solution.py:44
  164.6 58.8 %all-to-all-start = ((bf16[8,128,1024]{2,1,0:T(8,128)(2,1)}), bf16[8,128,1024]{2,1,0:T(8,128)(2,1)}, u32[]{:S(2)}, u32[]{:S(2)}) async-start(bf16[8,128,1024]{2,1,0:T(8,128)(2,1)} %stack.2), calls=%async_computation.2 | async-start | bytes 4194304 | tf_op jit(solution)/shard_map/all_to_all | solution.py:51
  172.4 187.5 %reduce-scatter.16.cloned.1.call-start = ((), (), s32[]{:S(2)}) async-start(), calls=%async_computation.12 | async-start | bytes 2162688
  223.3 1.2 copy-start.3
  223.3 230.0 %reduce-scatter.14.cloned.1.call-start = ((), (), s32[]{:S(2)}) async-start(), calls=%async_computation.10 | async-start | bytes 2162688 | tf_op jit(solution)/shard_map/reduce_scatter | solution.py:63
  228.8 318.0 %reduce-scatter.18.cloned.1.call-start = ((), (), s32[]{:S(2)}) async-start(), calls=%async_computation.13 | async-start | bytes 2162688
  270.2 1.2 copy-start.1
  270.2 400.4 %reduce-scatter.10.cloned.1.call-start = ((), (), s32[]{:S(2)}) async-start(), calls=%async_computation.7 | async-start | bytes 8650752 | tf_op jit(solution)/shard_map/reduce_scatter | solution.py:40
Sparse Core Ops, SparseCore 0:
  9.8 95.2 all-gather.3
  118.8 43.2 reduce-scatter.11
  163.9 54.3 all-gather.5
  219.9 42.6 all-gather.7
  266.8 93.0 reduce-scatter.15
  364.2 89.0 reduce-scatter.13
  457.7 89.1 reduce-scatter.17
  551.4 119.1 reduce-scatter.9
